TPU v7x, 32 devices: a whole 2x2x4 slice. The times are simulated.
32 devices in a mesh: stream: 2 (over x), batch: 4 (over y, core), tensor: 4 (over z).
Axes of the slice: x: 2, y: 2, z: 4, core: 2. Of those that a mesh axis runs over, the one named last changes fastest.
Arguments:
- hidden: bfloat16 [2, 3072, 768], P('stream', 'batch'), may hold values from -6 to 6
- cotangent: bfloat16 [2, 3072, 768], P('stream', 'batch'), may hold values from -6 to 6
- qkv_weight: bfloat16 [2, 768, 2304], P('stream', None, 'tensor'), may hold values from -0.21875 to 0.21875
- proj_weight: bfloat16 [2, 768, 768], P('stream', 'tensor'), may hold values from -1.75 to 1.75
- up_weight: bfloat16 [2, 768, 3072], P('stream', None, 'tensor'), may hold values from -0.21875 to 0.21875
- down_weight: bfloat16 [2, 3072, 768], P('stream', 'tensor'), may hold values from -0.109375 to 0.109375
- query_value_bias: bfloat16 [1536], P('tensor'), may hold values from -2 to 2
- unit_bias: bfloat16 [3072], P('tensor'), may hold values from -2 to 2
- layer_gain: bfloat16 [2, 768], replicated, may hold values from 0.5 to 1.5
- layer_shift: bfloat16 [2, 768], replicated, may hold values from -2 to 2
- output_bias: bfloat16 [2, 768], replicated, may hold values from -2 to 2
- scale_gain: bfloat16 [3, 768], replicated, may hold values from 0.5 to 1.5
- position_bias: bfloat16 [12, 32], P('tensor'), may hold values from -4 to 4
- cross_query: bfloat16 [768, 768], P(None, 'tensor'), may hold values from -0.21875 to 0.21875
- cross_key_value: bfloat16 [768, 1536], P(None, 'tensor'), may hold values from -0.21875 to 0.21875
- cross_proj: bfloat16 [768, 768], P('tensor'), may hold values from -1.75 to 1.75
- encodings: float32 [4, 768, 768], P('batch'), may hold values from -6 to 6
- query_vectors: float32 [4, 768], P('batch'), may hold values from -9 to 9
- passage_lengths: int32 [4, 2], P('batch'), may hold values from 1 to 384, as said below
- target_lengths: int32 [4], P('batch'), may hold values from 1 to 768, as said below
Outputs:
- block_out: bfloat16 [2, 3072, 768], P('stream', 'batch')
- input_grad: float32 [2, 3072, 768], P('stream', 'batch')
- grad_qkv: float32 [2, 768, 2304], P('stream', None, 'tensor')
- grad_proj: float32 [2, 768, 768], P('stream', 'tensor')
- grad_up: float32 [2, 768, 3072], P('stream', None, 'tensor')
- grad_down: float32 [2, 3072, 768], P('stream', 'tensor')
- grad_query_value_bias: float32 [1536], P('tensor')
- grad_unit_bias: float32 [3072], P('tensor')
- grad_layer_gain: float32 [2, 768], replicated
- grad_layer_shift: float32 [2, 768], replicated
- grad_output_bias: float32 [2, 768], replicated
- grad_scale_gain: float32 [3, 768], replicated
- grad_position_bias: float32 [12, 32], P('tensor')
- grad_cross_query: float32 [768, 768], P(None, 'tensor')
- grad_cross_key_value: float32 [768, 1536], P(None, 'tensor')
- grad_cross_proj: float32 [768, 768], P('tensor')
- retrieval_loss: float32 [4], P('batch')
Inputs may be any that keep to these rules, and one draw needn't show every extreme that they name: `passage_lengths`: A passage's valid tokens are its first ones; some passage has all 384. `target_lengths`: A query's valid target rows are its first ones; some query has all 768.
All inputs are finite; a program needn't handle non-finite values.
Results may differ from a plain program's by a relative error of at most 0.03.
Values may be sent and summed in bfloat16 or wider, within the bound.
A program may use at most 128 MiB of HBM per device.

v0:
```python
from functools import partial

import jax
import jax.numpy as jnp
import numpy as np
from jax import lax
from jax.sharding import PartitionSpec as P

HEADS = 12
HEAD_DIM = 64
PLEN = 384
NPASS = 2
SEQ = 768


EPS = 1e-06
NEG = -1000000000.0
HIGH = lax.Precision.HIGHEST


def from_behind(value, axis, steps):
    count = lax.axis_size(axis)
    first, last = (max(0, -steps), min(count, count - steps))
    return lax.ppermute(value, axis, [(source, source + steps) for source in range(first, last)])


def offset_onehot(length, buckets):
    exact = buckets // 2
    distance = np.arange(length)
    far_bucket = exact + (
        np.log(np.maximum(distance, 1) / exact) / np.log(128.0 / exact) * (buckets - exact)
    ).astype(np.int64)
    near_table = np.where(distance < exact, distance, np.minimum(far_bucket, buckets - 1))
    column = np.arange(2 * length)
    column_bucket = near_table[np.maximum(length - 1 - column, 0)]
    return (column_bucket[None, :] == np.arange(buckets)[:, None]).astype(np.float32)


def layer_norm_forward(values, norm_gain, norm_shift):
    centered = values - jnp.mean(values, axis=-1, keepdims=True)
    inv_root = lax.rsqrt(jnp.mean(centered * centered, axis=-1, keepdims=True) + EPS)
    normed = centered * inv_root
    return (normed * norm_gain + norm_shift, normed, inv_root)


def layer_norm_backward(normed, inv_root, norm_gain, upstream):
    scaled_up = upstream * norm_gain
    grad_in = inv_root * (
        scaled_up
        - jnp.mean(scaled_up, axis=-1, keepdims=True)
        - normed * jnp.mean(scaled_up * normed, axis=-1, keepdims=True)
    )
    return (grad_in, jnp.sum(upstream * normed, axis=0), jnp.sum(upstream, axis=0))


def rms_forward(values, norm_gain):
    inv_root = lax.rsqrt(jnp.mean(values * values, axis=-1, keepdims=True) + EPS)
    return (values * inv_root * norm_gain, inv_root)


def rms_backward(values, inv_root, norm_gain, upstream):
    scaled_up = upstream * norm_gain
    grad_in = inv_root * scaled_up - values * (inv_root * inv_root * inv_root) * jnp.mean(
        scaled_up * values, axis=-1, keepdims=True
    )
    return (grad_in, jnp.sum(upstream * (values * inv_root), axis=0))


def gelu_back(pre_act, upstream):
    _, pull = jax.vjp(partial(jax.nn.gelu, approximate=True), pre_act)
    return pull(upstream)[0]


def passage_keys(pass_lens):
    return (jnp.arange(PLEN)[None, :] < pass_lens[:, None]).reshape(SEQ)


def self_mask(is_first, pass_lens, target_len):
    row_index = jnp.arange(SEQ)[:, None]
    col_index = jnp.arange(SEQ)[None, :]
    within = (row_index // PLEN == col_index // PLEN) & passage_keys(pass_lens)[None, :]
    causal = (col_index <= row_index) & (col_index < target_len)
    return jnp.where(is_first, within, causal)


def cross_mask(pass_lens):
    return jnp.broadcast_to(passage_keys(pass_lens)[None, :], (SEQ, SEQ))


def attend_scores(queries, key_heads, score_bias, allowed):
    scores = (
        jnp.einsum("ihd,jhd->hij", queries, key_heads, preferred_element_type=jnp.float32)
        * HEAD_DIM ** (-0.5)
        + score_bias
    )
    return jnp.where(allowed, scores, NEG)


def attend_forward(queries, key_heads, values, score_bias, allowed):
    scores = attend_scores(queries, key_heads, score_bias, allowed)
    row_max = jnp.max(scores, axis=-1, keepdims=True)
    exp_scores = jnp.exp(scores - row_max)
    total_sum = jnp.sum(exp_scores, axis=-1, keepdims=True)
    attn_probs = exp_scores / total_sum
    mixed_out = jnp.einsum(
        "hij,jhd->ihd", attn_probs.astype(jnp.bfloat16), values, preferred_element_type=jnp.float32
    )
    return (mixed_out.astype(jnp.bfloat16), row_max + jnp.log(total_sum), attn_probs)


def attend_backward(queries, key_heads, values, score_bias, allowed, log_norm, grad_mixed):
    attn_probs = jnp.exp(attend_scores(queries, key_heads, score_bias, allowed) - log_norm)
    grad_probs = jnp.einsum("ihd,jhd->hij", grad_mixed, values, preferred_element_type=jnp.float32)
    grad_s = (
        attn_probs * (grad_probs - jnp.sum(attn_probs * grad_probs, axis=-1, keepdims=True))
    ).astype(jnp.bfloat16)
    grad_q = jnp.einsum(
        "hij,jhd->ihd", grad_s, key_heads, preferred_element_type=jnp.float32
    ) * HEAD_DIM ** (-0.5)
    grad_k = jnp.einsum(
        "hij,ihd->jhd", grad_s, queries, preferred_element_type=jnp.float32
    ) * HEAD_DIM ** (-0.5)
    grad_v = jnp.einsum(
        "hij,ihd->jhd",
        attn_probs.astype(jnp.bfloat16),
        grad_mixed,
        preferred_element_type=jnp.float32,
    )
    return (grad_q, grad_k, grad_v, grad_s)


def sum_units(unit_pair):
    return (
        lax.psum(unit_pair[0].astype(jnp.bfloat16), "batch").astype(jnp.float32),
        lax.psum(unit_pair[1].astype(jnp.bfloat16), "batch").astype(jnp.float32),
    )


def sum_heads(head_pair):
    return (
        lax.psum(head_pair[0].astype(jnp.bfloat16), "batch").astype(jnp.float32),
        lax.psum(head_pair[1].astype(jnp.bfloat16), "batch").astype(jnp.float32),
    )


def local(
    hidden,
    cotangent,
    qkv_weight,
    proj_weight,
    up_weight,
    down_weight,
    query_value_bias,
    unit_bias,
    layer_gain,
    layer_shift,
    output_bias,
    scale_gain,
    position_bias,
    cross_query,
    cross_key_value,
    cross_proj,
    encodings,
    query_vectors,
    passage_lengths,
    target_lengths,
):
    is_first = lax.axis_index("stream") == 0
    local_heads = proj_weight.shape[1] // HEAD_DIM
    query_count = query_vectors.shape[0]
    total_rows = hidden.shape[1]
    width = hidden.shape[2]
    source = hidden[0].astype(jnp.float32)
    qkv_local = qkv_weight[0]
    proj_local = proj_weight[0]
    up_local = up_weight[0]
    down_local = down_weight[0]
    gains = scale_gain.astype(jnp.float32)
    norm_gain = layer_gain.astype(jnp.float32)
    norm_shift = layer_shift.astype(jnp.float32)
    out_shift = jnp.where(is_first, output_bias.astype(jnp.float32), 0.0)
    value_heads = query_value_bias.astype(jnp.float32).reshape(local_heads, 2, HEAD_DIM)
    packed_shift = jnp.stack(
        [value_heads[:, 0], jnp.zeros_like(value_heads[:, 0]), value_heads[:, 1]], axis=1
    ).reshape(-1)
    packed_shift = jnp.where(is_first, packed_shift, 0.0)
    unit_shift = jnp.where(is_first, unit_bias, jnp.zeros_like(unit_bias))
    onehot_cols = jnp.asarray(offset_onehot(SEQ, position_bias.shape[1]))
    position_f32 = position_bias.astype(jnp.float32)

    def lookup(table_values):
        diagonal = jnp.dot(
            table_values, onehot_cols, precision=HIGH, preferred_element_type=jnp.float32
        )
        repeated = jnp.tile(diagonal, (1, SEQ))
        band = repeated[:, SEQ - 1 : SEQ - 1 + SEQ * (2 * SEQ - 1)].reshape(
            table_values.shape[0], SEQ, 2 * SEQ - 1
        )
        return band[:, :, :SEQ]

    self_bias = jnp.where(is_first, 0.0, lookup(position_f32))
    enc_low = encodings.astype(jnp.bfloat16).reshape(total_rows, width)
    pre_normed, pre_root = rms_forward(source, gains[0])
    first_in = jnp.where(is_first, source, pre_normed).astype(jnp.bfloat16)
    packed = (
        jnp.dot(first_in, qkv_local, preferred_element_type=jnp.float32) + packed_shift
    ).astype(jnp.bfloat16)
    packed = packed.reshape(query_count, SEQ, local_heads, 3, HEAD_DIM)

    def self_forward(query_items):
        packed_query, pass_lens, target_len = query_items
        allowed = self_mask(is_first, pass_lens, target_len)
        mixed_out, log_norm, _ = attend_forward(
            packed_query[:, :, 0], packed_query[:, :, 1], packed_query[:, :, 2], self_bias, allowed
        )
        return (mixed_out, log_norm)

    self_mixed, self_norm = lax.map(self_forward, (packed, passage_lengths, target_lengths))
    self_flat = self_mixed.reshape(total_rows, -1)
    attn_out = (
        lax.psum(
            jnp.dot(self_flat, proj_local, preferred_element_type=jnp.float32).astype(jnp.bfloat16),
            "tensor",
        ).astype(jnp.float32)
        + out_shift[0]
    )
    first_sum = source + attn_out
    first_norm, first_normed, first_root = layer_norm_forward(
        first_sum, norm_gain[0], norm_shift[0]
    )
    middle = jnp.where(is_first, first_norm, first_sum)

    def cross_run(middle_in):
        normed, inv_root = rms_forward(middle_in, gains[1])
        normed_low = normed.astype(jnp.bfloat16)
        cross_queries = (
            jnp.dot(normed_low, cross_query, preferred_element_type=jnp.float32)
            .astype(jnp.bfloat16)
            .reshape(query_count, SEQ, local_heads, HEAD_DIM)
        )
        cross_keys = (
            jnp.dot(enc_low, cross_key_value, preferred_element_type=jnp.float32)
            .astype(jnp.bfloat16)
            .reshape(query_count, SEQ, local_heads, 2, HEAD_DIM)
        )

        def per_query(query_items):
            query_block, key_block, pass_lens, target_len = query_items
            mixed_out, log_norm, attn_probs = attend_forward(
                query_block, key_block[:, :, 0], key_block[:, :, 1], 0.0, cross_mask(pass_lens)
            )
            live_rows = (jnp.arange(SEQ) < target_len).astype(jnp.float32)
            column_mass = jnp.sum(attn_probs * live_rows[None, :, None], axis=(0, 1))
            return (mixed_out, log_norm, jnp.sum(column_mass.reshape(NPASS, PLEN), axis=1))

        cross_mixed, cross_norm, cross_mass = lax.map(
            per_query, (cross_queries, cross_keys, passage_lengths, target_lengths)
        )
        partial_out = jnp.dot(
            cross_mixed.reshape(total_rows, -1), cross_proj, preferred_element_type=jnp.float32
        )
        return (
            partial_out,
            cross_mass,
            normed_low,
            inv_root,
            cross_queries,
            cross_keys,
            cross_mixed,
            cross_norm,
        )

    def cross_skip(middle_in):
        head_zero = jnp.zeros((query_count, SEQ, local_heads, HEAD_DIM), jnp.bfloat16)
        return (
            jnp.zeros((total_rows, width), jnp.float32),
            jnp.zeros((query_count, NPASS), jnp.float32),
            jnp.zeros((total_rows, width), jnp.bfloat16),
            jnp.zeros((total_rows, 1), jnp.float32),
            head_zero,
            jnp.zeros((query_count, SEQ, local_heads, 2, HEAD_DIM), jnp.bfloat16),
            head_zero,
            jnp.zeros((query_count, local_heads, SEQ, 1), jnp.float32),
        )

    (
        cross_part,
        cross_mass,
        cross_normed,
        cross_root,
        cross_queries,
        cross_keys,
        cross_mixed,
        cross_norm,
    ) = lax.cond(is_first, cross_skip, cross_run, middle)
    cross_total, mass_total = (
        lax.psum(cross_part.astype(jnp.bfloat16), "tensor").astype(jnp.float32),
        lax.psum(cross_mass.astype(jnp.bfloat16), "tensor").astype(jnp.float32),
    )
    second = middle + cross_total
    ffn_normed, ffn_root = rms_forward(second, gains[2])
    ffn_in = jnp.where(is_first, second, ffn_normed).astype(jnp.bfloat16)
    pre_act = jnp.dot(ffn_in, up_local, preferred_element_type=jnp.float32) + unit_shift.astype(
        jnp.float32
    )
    act_low = jax.nn.gelu(pre_act, approximate=True).astype(jnp.bfloat16)
    unit_out = lax.psum(
        jnp.dot(act_low, down_local, preferred_element_type=jnp.float32).astype(jnp.bfloat16),
        "tensor",
    ).astype(jnp.float32)
    unit_out = unit_out + out_shift[1]
    final_sum = second + unit_out
    final_norm, final_normed, final_root = layer_norm_forward(
        final_sum, norm_gain[1], norm_shift[1]
    )
    result = jnp.where(is_first, final_norm, final_sum)
    live_keys = (jnp.arange(PLEN)[None, None, :] < passage_lengths[:, :, None]).astype(jnp.float32)
    pass_count = passage_lengths.astype(jnp.float32)
    pooled = (
        jnp.sum(result.reshape(query_count, NPASS, PLEN, width) * live_keys[..., None], axis=2)
        / pass_count[..., None]
    )
    scores = jnp.sum(pooled * query_vectors[:, None, :], axis=-1)
    incoming = from_behind(scores, "stream", 1)
    reader_targets = mass_total / (HEADS * target_lengths.astype(jnp.float32))[:, None]
    targets = jnp.where(is_first, 1.0 / NPASS, reader_targets)
    log_probs = jax.nn.log_softmax(incoming, axis=-1)
    own_loss = jnp.sum(targets * (jnp.log(targets) - log_probs), axis=-1)
    own_score_grad = jnp.exp(log_probs) * jnp.sum(targets, axis=-1, keepdims=True) - targets
    back_grad, back_loss = from_behind((own_score_grad, own_loss), "stream", -1)
    score_grad = jnp.where(is_first, back_grad, own_score_grad)
    kl_loss = jnp.where(is_first, back_loss, own_loss)
    upstream = cotangent[0].astype(jnp.float32)
    pooled_grad = score_grad[..., None] * query_vectors[:, None, :] / pass_count[..., None]
    row_grad = (pooled_grad[:, :, None, :] * live_keys[..., None]).reshape(total_rows, width)
    upstream = upstream + jnp.where(is_first, row_grad, 0.0)
    final_back, gain_grad_two, shift_grad_two = layer_norm_backward(
        final_normed, final_root, norm_gain[1], upstream
    )
    final_grad = jnp.where(is_first, final_back, upstream)
    unit_grad = final_grad.astype(jnp.bfloat16)
    out_grad_two = jnp.sum(unit_grad.astype(jnp.float32), axis=0)
    act_grad = jnp.dot(unit_grad, down_local.T, preferred_element_type=jnp.float32)
    pre_grad = gelu_back(pre_act, act_grad).astype(jnp.bfloat16)
    up_grad = jnp.dot(ffn_in.T, pre_grad, preferred_element_type=jnp.float32)
    down_grad = jnp.dot(act_low.T, unit_grad, preferred_element_type=jnp.float32)
    shift_grad = jnp.sum(pre_grad.astype(jnp.float32), axis=0)
    ffn_in_grad = lax.psum(
        jnp.dot(pre_grad, up_local.T, preferred_element_type=jnp.float32).astype(jnp.bfloat16),
        "tensor",
    ).astype(jnp.float32)
    unit_pair = (up_grad, down_grad)
    ffn_back, rms_grad_three = rms_backward(second, ffn_root, gains[2], ffn_in_grad)
    second_grad = final_grad + jnp.where(is_first, ffn_in_grad, ffn_back)

    def cross_back_run(grad_in):
        cross_grad = grad_in.astype(jnp.bfloat16)
        proj_grad = jnp.dot(
            cross_mixed.reshape(total_rows, -1).T, cross_grad, preferred_element_type=jnp.float32
        )
        mixed_grad = (
            jnp.dot(cross_grad, cross_proj.T, preferred_element_type=jnp.float32)
            .astype(jnp.bfloat16)
            .reshape(query_count, SEQ, local_heads, HEAD_DIM)
        )

        def per_query(query_items):
            query_block, key_block, pass_lens, log_norm, grad_block = query_items
            grad_q, grad_k, grad_v, _ = attend_backward(
                query_block,
                key_block[:, :, 0],
                key_block[:, :, 1],
                0.0,
                cross_mask(pass_lens),
                log_norm,
                grad_block,
            )
            return (grad_q, jnp.stack([grad_k, grad_v], axis=2))

        query_grad, pair_grad = lax.map(
            per_query, (cross_queries, cross_keys, passage_lengths, cross_norm, mixed_grad)
        )
        query_grad = query_grad.astype(jnp.bfloat16).reshape(total_rows, -1)
        pair_grad = pair_grad.astype(jnp.bfloat16).reshape(total_rows, -1)
        in_part = jnp.dot(query_grad, cross_query.T, preferred_element_type=jnp.float32)
        query_weight_grad = jnp.dot(cross_normed.T, query_grad, preferred_element_type=jnp.float32)
        pair_weight_grad = jnp.dot(enc_low.T, pair_grad, preferred_element_type=jnp.float32)
        return (in_part, query_weight_grad, pair_weight_grad, proj_grad)

    def cross_back_skip(grad_in):
        return (
            jnp.zeros((total_rows, width), jnp.float32),
            jnp.zeros(cross_query.shape, jnp.float32),
            jnp.zeros(cross_key_value.shape, jnp.float32),
            jnp.zeros(cross_proj.shape, jnp.float32),
        )

    cross_in_part, cross_query_grad, cross_pair_grad, cross_proj_grad = lax.cond(
        is_first, cross_back_skip, cross_back_run, second_grad
    )
    cross_in_grad = lax.psum(cross_in_part.astype(jnp.bfloat16), "tensor").astype(jnp.float32)
    cross_back, rms_grad_two = rms_backward(middle, cross_root, gains[1], cross_in_grad)
    middle_grad = second_grad + jnp.where(is_first, 0.0, cross_back)
    first_back, gain_grad_one, shift_grad_one = layer_norm_backward(
        first_normed, first_root, norm_gain[0], middle_grad
    )
    first_grad = jnp.where(is_first, first_back, middle_grad)
    attn_grad = first_grad.astype(jnp.bfloat16)
    out_grad_one = jnp.sum(attn_grad.astype(jnp.float32), axis=0)
    proj_weight_grad = jnp.dot(self_flat.T, attn_grad, preferred_element_type=jnp.float32)
    self_grad = (
        jnp.dot(attn_grad, proj_local.T, preferred_element_type=jnp.float32)
        .astype(jnp.bfloat16)
        .reshape(query_count, SEQ, local_heads, HEAD_DIM)
    )
    _, lookup_pull = jax.vjp(lookup, position_f32)

    def self_backward(query_items):
        packed_query, pass_lens, target_len, log_norm, grad_block = query_items
        allowed = self_mask(is_first, pass_lens, target_len)
        grad_q, grad_k, grad_v, grad_s = attend_backward(
            packed_query[:, :, 0],
            packed_query[:, :, 1],
            packed_query[:, :, 2],
            self_bias,
            allowed,
            log_norm,
            grad_block,
        )
        return (
            jnp.stack([grad_q, grad_k, grad_v], axis=2),
            lookup_pull(grad_s.astype(jnp.float32))[0],
        )

    packed_grad, table_grads = lax.map(
        self_backward, (packed, passage_lengths, target_lengths, self_norm, self_grad)
    )
    packed_grad = packed_grad.astype(jnp.bfloat16).reshape(total_rows, -1)
    table_grad = jnp.sum(table_grads, axis=0)
    qkv_weight_grad = jnp.dot(first_in.T, packed_grad, preferred_element_type=jnp.float32)
    shift_heads = jnp.sum(packed_grad.astype(jnp.float32), axis=0).reshape(local_heads, 3, HEAD_DIM)
    value_bias_grad = jnp.stack([shift_heads[:, 0], shift_heads[:, 2]], axis=1).reshape(-1)
    first_in_grad = lax.psum(
        jnp.dot(packed_grad, qkv_local.T, preferred_element_type=jnp.float32).astype(jnp.bfloat16),
        "tensor",
    ).astype(jnp.float32)
    pre_back, rms_grad_one = rms_backward(source, pre_root, gains[0], first_in_grad)
    input_grad = first_grad + jnp.where(is_first, first_in_grad, pre_back)
    qkv_sum, proj_sum = sum_heads((qkv_weight_grad, proj_weight_grad))
    up_sum, down_sum = sum_units(unit_pair)

    def retriever_only(values):
        return jnp.where(is_first, values, 0.0)

    def reader_only(values):
        return jnp.where(is_first, 0.0, values)

    side_terms = (
        retriever_only(value_bias_grad),
        retriever_only(shift_grad),
        retriever_only(jnp.stack([gain_grad_one, gain_grad_two])),
        retriever_only(jnp.stack([shift_grad_one, shift_grad_two])),
        retriever_only(jnp.stack([out_grad_one, out_grad_two])),
        reader_only(jnp.stack([rms_grad_one, rms_grad_two, rms_grad_three])),
        reader_only(table_grad),
        cross_query_grad,
        cross_pair_grad,
        cross_proj_grad,
    )
    (
        value_sum,
        unit_bias_sum,
        gain_sum,
        shift_sum,
        out_sum,
        scale_sum,
        table_sum,
        cross_query_sum,
        cross_pair_sum,
        cross_proj_sum,
    ) = lax.psum(
        (
            side_terms[0],
            side_terms[1],
            side_terms[2],
            side_terms[3],
            side_terms[4],
            side_terms[5],
            side_terms[6],
            side_terms[7],
            side_terms[8],
            side_terms[9],
        ),
        ("stream", "batch"),
    )
    return (
        result.astype(jnp.bfloat16)[None],
        input_grad[None],
        qkv_sum[None],
        proj_sum[None],
        up_sum[None],
        down_sum[None],
        value_sum,
        unit_bias_sum,
        gain_sum,
        shift_sum,
        out_sum,
        scale_sum,
        table_sum,
        cross_query_sum,
        cross_pair_sum,
        cross_proj_sum,
        kl_loss,
    )


def solution(mesh):
    in_specs = (
        P("stream", "batch", None),
        P("stream", "batch", None),
        P("stream", None, "tensor"),
        P("stream", "tensor", None),
        P("stream", None, "tensor"),
        P("stream", "tensor", None),
        P("tensor"),
        P("tensor"),
        P(),
        P(),
        P(),
        P(),
        P("tensor", None),
        P(None, "tensor"),
        P(None, "tensor"),
        P("tensor", None),
        P("batch", None, None),
        P("batch", None),
        P("batch", None),
        P("batch"),
    )
    out_specs = (
        P("stream", "batch", None),
        P("stream", "batch", None),
        P("stream", None, "tensor"),
        P("stream", "tensor", None),
        P("stream", None, "tensor"),
        P("stream", "tensor", None),
        P("tensor"),
        P("tensor"),
        P(),
        P(),
        P(),
        P(),
        P("tensor", None),
        P(None, "tensor"),
        P(None, "tensor"),
        P("tensor", None),
        P("batch"),
    )
    return jax.shard_map(local, mesh=mesh, in_specs=in_specs, out_specs=out_specs, check_vma=False)
```

profile of v0, /device:TPU:0, one launch (start us, length us, event | category | flops | bytes accessed | tf_op | source)
XLA Modules:
  0.0 782.8 jit_solution(4818526009258459693)
XLA Ops:
  18.1 29.7 %copy.165 = f32[1,3,768,1536]{3,1,2,0:T(4,128)S(1)} copy(f32[1,3,768,1536]{3,2,1,0:T(8,128)S(1)} %broadcast_bitcast_fusion) | data formatting | bytes 28311552
  47.8 13.0 %slice.114 = f32[3,1178880]{1,0:T(4,128)} slice(f32[3,1179648]{1,0:T(4,128)S(1)} %bitcast.279), slice={[0:3], [767:1179647]} | slice | bytes 28293120 | tf_op jit(solution)/shard_map/slice | solution.py:196
  60.9 40.8 %reshape.690 = f32[3536640]{0:T(1024)} reshape(f32[3,1178880]{1,0:T(4,128)} %slice.114) | data formatting | bytes 28293120
  101.7 23.3 %reshape.662 = f32[3,768,1535]{2,1,0:T(8,128)} reshape(f32[3536640]{0:T(1024)} %reshape.690) | data formatting | bytes 28293120 | tf_op jit(solution)/shard_map/reshape | solution.py:196
  125.0 6.3 slice.115
  131.3 8.4 %copy.163 = f32[3,768,768]{1,2,0:T(8,128)} copy(f32[3,768,768]{2,1,0:T(8,128)} %slice.115) | data formatting | bytes 14155776
  155.1 57.3 %all-reduce.14.cloned.1.call-done = bf16[768,768]{1,0:T(8,128)(2,1)} async-done(((bf16[768,768]{1,0:T(8,128)(2,1)}), bf16[768,768]{1,0:T(8,128)(2,1)}) %all-reduce.14.cloned.1.call-update) | async-done | bytes 1179664 | tf_op jit(solution)/shard_map/psum | solution.py:221
  215.8 6.1 conditional.2
  223.3 73.7 %all-reduce.16.cloned.1.call-done = bf16[768,768]{1,0:T(8,128)(2,1)} async-done(((bf16[768,768]{1,0:T(8,128)(2,1)}), bf16[768,768]{1,0:T(8,128)(2,1)}) %all-reduce.16.cloned.1.call-update) | async-done | bytes 1179664 | tf_op jit(solution)/shard_map/psum | solution.py:297
  309.1 11.3 %psum.150 = bf16[1,2]{1,0:T(2,128)(2,1)} all-reduce(bf16[1,2]{1,0:T(2,128)(2,1)} %get-tuple-element.189), channel_id=1, replica_groups=mesh['stream'=2,'batch'=4,'tensor'=4] {'tensor'}, use_global_device_ids=true, to_apply=%region_22.23 | all-reduce | flops 2 | bytes 8 | tf_op jit(solution)/shard_map/psum | solution.py:298
  320.4 40.8 %all-reduce.18.cloned.1.call-done = bf16[768,768]{1,0:T(8,128)(2,1)} async-done(((bf16[768,768]{1,0:T(8,128)(2,1)}), bf16[768,768]{1,0:T(8,128)(2,1)}) %all-reduce.18.cloned.1.call-update) | async-done | bytes 1179664 | tf_op jit(solution)/shard_map/psum | solution.py:307
  398.3 54.5 %all-reduce.20.cloned.1.call-done = bf16[768,768]{1,0:T(8,128)(2,1)} async-done(((bf16[768,768]{1,0:T(8,128)(2,1)}), bf16[768,768]{1,0:T(8,128)(2,1)}) %all-reduce.20.cloned.1.call-update) | async-done | bytes 1179664 | tf_op jit(solution)/shard_map/psum | solution.py:348
  466.8 73.3 %all-reduce.22.cloned.1.call-done = bf16[768,768]{1,0:T(8,128)(2,1)} async-done(((bf16[768,768]{1,0:T(8,128)(2,1)}), bf16[768,768]{1,0:T(8,128)(2,1)}) %all-reduce.22.cloned.1.call-update) | async-done | bytes 1179664 | tf_op jit(solution)/shard_map/psum | solution.py:401
  543.1 4.3 multiply_reduce_fusion.4
  556.8 4.3 multiply_convert_fusion.2
  591.1 6.1 copy.164
  599.0 5.6 pad.10.clone
  604.6 13.4 %reshape.692 = bf16[3536640]{0:T(1024)(128)(2,1)} reshape(bf16[3,768,1535]{2,1,0:T(8,128)(2,1)} %pad.10.clone) | data formatting | bytes 14146560
  618.0 10.6 %reshape.666 = bf16[3,1178880]{1,0:T(4,128)(2,1)} reshape(bf16[3536640]{0:T(1024)(128)(2,1)} %reshape.692) | data formatting | bytes 14146560 | tf_op jit(solution)/shard_map/while/body/eval_jaxpr/transpose(jvp())/reshape | solution.py:196
  628.6 11.7 %pad_convert_fusion = f32[3,1179648]{1,0:T(4,128)} fusion(bf16[3,1178880]{1,0:T(4,128)(2,1)} %reshape.666), kind=kLoop, calls=%fused_computation.53 | loop fusion | flops 3538944 | bytes 21229056 | tf_op jit(solution)/shard_map/while/body/eval_jaxpr/transpose(jvp())/reshape | solution.py:195
  640.4 10.3 %bitcast_reduce_fusion = f32[3,1536]{1,0:T(4,128)S(1)} fusion(f32[1,3,768,1536]{3,1,2,0:T(4,128)} %bitcast.278), kind=kLoop, calls=%fused_computation.52 | loop fusion | flops 3534336 | bytes 14174208 | tf_op jit(solution)/shard_map/while/body/eval_jaxpr/transpose(jvp())/reduce_sum | solution.py:195
  658.5 24.3 %all-reduce.2 = (f32[384]{0:T(512)}, f32[768]{0:T(1024)}, f32[2,768]{1,0:T(2,128)}, f32[2,768]{1,0:T(2,128)}, f32[2,768]{1,0:T(2,128)}, /*index=5*/f32[3,768]{1,0:T(4,128)}, f32[3,32]{1,0:T(4,128)}) all-reduce(f32[384]{0:T(512)} %select_n.238, ...), channel_id=1, replica_groups=mesh['stream'=2,'batch'=4,'tensor'=4] {'stream','batch'}, use_global_device_ids=true, to_apply=%region_43.44 | all-reduce | flops 8160 | bytes 65280 | tf_op jit(solution)/shard_map/psum | solution.py:481
  687.0 14.9 %all-reduce.28.cloned.1.call-done = (bf16[1,768,576]{1,2,0:T(8,128)(2,1)}, bf16[1,192,768]{2,1,0:T(8,128)(2,1)}, bf16[1,768,768]{2,1,0:T(8,128)(2,1)}, bf16[1,768,768]{2,1,0:T(8,128)(2,1)}) async-done(((bf16[1,768,576]{1,2,0:T(8,128)(2,1)}, bf16[1,192,768]{2,1,0:T(8,128)(2,1)}, bf16[1,768,768]{2,1,0:T(8,128)(2,1)}, bf16[1,768,768]{2,1,0:T(8,128)(2,1)}), (bf16[1,768,576]{1,2,0:T(8,128)(2,1)}, ...) | async-done | bytes 3538960 | tf_op jit(solution)/shard_map/psum | solution.py:141
  709.6 59.9 %all-reduce.26.cloned.1.call-done = (f32[768,192]{0,1:T(8,128)}, f32[768,384]{1,0:T(8,128)}, f32[192,768]{1,0:T(8,128)}) async-done(((f32[768,192]{0,1:T(8,128)}, f32[768,384]{1,0:T(8,128)}, f32[192,768]{1,0:T(8,128)}), (f32[768,192]{0,1:T(8,128)}, f32[768,384]{1,0:T(8,128)}, f32[192,768]{1,0:T(8,128)})) %all-reduce.26.cloned.1.call-update) | async-done | bytes 2359312 | tf_op jit(solution)/shard_map/psum | solution.py:481
  (350 shorter events, 168.4 us)
Async XLA Ops:
  7.2 295.5 %copy-start = (bf16[1,768,768]{2,1,0:T(8,128)(2,1)S(1)}, bf16[1,768,768]{2,1,0:T(8,128)(2,1)}, u32[]{:S(2)}) copy-start(bf16[1,768,768]{2,1,0:T(8,128)(2,1)} %param.30) | copy-start | bytes 3538948
  7.2 205.2 %all-reduce.14.cloned.1.call-start = ((), (), s32[]{:S(2)}) async-start(), calls=%async_computation | async-start | bytes 2359296 | tf_op jit(solution)/shard_map/psum | solution.py:221
  11.2 128.4 %copy-start.57 = (f32[768]{0:T(1024)}, f32[768]{0:T(1024)S(1)}, u32[]{:S(2)}) copy-start(f32[768]{0:T(1024)S(1)} %get-tuple-element.356) | copy-start | bytes 9220
  14.5 125.2 %copy-start.59 = (f32[768]{0:T(1024)}, f32[768]{0:T(1024)S(1)}, u32[]{:S(2)}) copy-start(f32[768]{0:T(1024)S(1)} %get-tuple-element.308) | copy-start | bytes 9220
  150.3 146.6 %all-reduce.16.cloned.1.call-start = ((), (), s32[]{:S(2)}) async-start(), calls=%async_computation.1 | async-start | bytes 2359296 | tf_op jit(solution)/shard_map/psum | solution.py:297
  151.0 64.0 %copy-start.47 = (f32[768]{0:T(1024)}, f32[768]{0:T(1024)S(1)}, u32[]{:S(2)}) copy-start(f32[768]{0:T(1024)S(1)} %get-tuple-element.310) | copy-start | bytes 9220
  221.9 139.2 %all-reduce.18.cloned.1.call-start = ((), (), s32[]{:S(2)}) async-start(), calls=%async_computation.2 | async-start | bytes 2359296 | tf_op jit(solution)/shard_map/psum | solution.py:307
  305.3 147.5 %all-reduce.20.cloned.1.call-start = ((), (), s32[]{:S(2)}) async-start(), calls=%async_computation.3 | async-start | bytes 2359296 | tf_op jit(solution)/shard_map/psum | solution.py:348
  366.8 4.7 collective-permute-start
  375.3 14.7 %copy-start.8 = (f32[768,768]{1,0:T(8,128)S(1)}, f32[768,768]{1,0:T(8,128)}, u32[]{:S(2)}) copy-start(f32[768,768]{1,0:T(8,128)} %copy-done.7) | copy-start | bytes 7077892
  375.4 14.7 %copy-start.24 = (bf16[1,768,768]{2,1,0:T(8,128)(2,1)S(1)}, bf16[1,768,768]{2,1,0:T(8,128)(2,1)}, u32[]{:S(2)}) copy-start(bf16[1,768,768]{2,1,0:T(8,128)(2,1)} %param.26) | copy-start | bytes 3538948
  375.4 14.7 %copy-start.46 = (f32[768]{0:T(1024)S(1)}, f32[768]{0:T(1024)}, u32[]{:S(2)}) copy-start(f32[768]{0:T(1024)} %copy-done.45) | copy-start | bytes 9220
  375.4 14.7 %copy-start.52 = (f32[768]{0:T(1024)S(1)}, f32[768]{0:T(1024)}, u32[]{:S(2)}) copy-start(f32[768]{0:T(1024)} %get-tuple-element.309) | copy-start | bytes 9220
  375.4 14.7 %copy-start.54 = (f32[768]{0:T(1024)S(1)}, f32[768]{0:T(1024)}, u32[]{:S(2)}) copy-start(f32[768]{0:T(1024)} %copy-done.53) | copy-start | bytes 9220
  375.4 14.7 %copy-start.70 = (f32[768]{0:T(1024)S(1)}, f32[768]{0:T(1024)}, u32[]{:S(2)}) copy-start(f32[768]{0:T(1024)} %convert_element_type.302) | copy-start | bytes 9220
  379.8 5.4 collective-permute-start.1
  395.9 56.9 %copy-start.62 = (f32[768]{0:T(1024)S(1)}, f32[768]{0:T(1024)}, u32[]{:S(2)}) copy-start(f32[768]{0:T(1024)} %copy-done.61) | copy-start | bytes 9220
  395.9 56.9 %copy-start.65 = (f32[768]{0:T(1024)S(1)}, f32[768]{0:T(1024)}, u32[]{:S(2)}) copy-start(f32[768]{0:T(1024)} %get-tuple-element.307) | copy-start | bytes 9220
  398.1 142.0 %all-reduce.22.cloned.1.call-start = ((), (), s32[]{:S(2)}) async-start(), calls=%async_computation.4 | async-start | bytes 2359296 | tf_op jit(solution)/shard_map/psum | solution.py:401
  464.4 78.6 %copy-start.5 = (bf16[1,768,768]{2,1,0:T(8,128)(2,1)S(1)}, bf16[1,768,768]{2,1,0:T(8,128)(2,1)}, u32[]{:S(2)}) copy-start(bf16[1,768,768]{2,1,0:T(8,128)(2,1)} %param.25) | copy-start | bytes 3538948
  464.4 191.0 %all-reduce.24.cloned.1.call-start = ((), (), s32[]{:S(2)}) async-start(), calls=%async_computation.5 | async-start | bytes 2359296 | tf_op jit(solution)/shard_map/psum | solution.py:443
  567.0 134.9 %all-reduce.28.cloned.1.call-start = ((), (), s32[]{:S(2)}) async-start(), calls=%async_computation.7 | async-start | bytes 7077888 | tf_op jit(solution)/shard_map/psum | solution.py:141
  576.5 192.9 %all-reduce.26.cloned.1.call-start = ((), (), s32[]{:S(2)}) async-start(), calls=%async_computation.6 | async-start | bytes 4718592 | tf_op jit(solution)/shard_map/psum | solution.py:481
  576.6 5.4 collective-permute-start.2
  (88 other events, 335.5 us)
Sparse Core Ops, SparseCore 0:
  150.5 61.9 all-reduce.13
  222.1 74.8 all-reduce.15
  305.5 55.6 all-reduce.17
  398.2 54.5 all-reduce.19
  464.5 75.4 all-reduce.21
  567.1 55.4 all-reduce.23
  626.3 75.5 all-reduce.27
  705.9 63.4 all-reduce.25
where the time goes:
time: 788 us; the launch traced here: 783 us
  waiting for transfers between devices  383 us (49%)
  local copies, waits for them, and re-layouts  198 us (25%)
  other arithmetic  102 us (13%)
  matrix products  36.4 us (5%)
  blocking collectives  35.5 us (5%)
  between operations  19.3 us (2%)
    unnamed x211, local copies, waits for them, and re-layouts  116 us
    psum x1, waiting for transfers between devices, local(): lax.psum(cross_part.astype(jnp.bfloat16), 'tensor').astype(jnp.float32)  73.7 us
    psum x1, waiting for transfers between devices, local(): lax.psum(cross_in_part.astype(jnp.bfloat16), 'tensor').astype(jnp.float32)  73.3 us
    psum x1, waiting for transfers between devices, local(): lax.psum((side_terms[0], side_terms[1], side_terms[2], side_terms[3], sid...  59.9 us
    psum x1, waiting for transfers between devices, local(): lax.psum(jnp.dot(self_flat, proj_local, preferred_element_type=jnp.float3...  57.3 us
    psum x1, waiting for transfers between devices, local(): lax.psum(jnp.dot(pre_grad, up_local.T, preferred_element_type=jnp.float32...  54.5 us
    psum x1, waiting for transfers between devices, local(): lax.psum(jnp.dot(act_low, down_local, preferred_element_type=jnp.float32)...  40.8 us
    reshape x2, local copies, waits for them, and re-layouts, lookup(): repeated[:, SEQ - 1:SEQ - 1 + SEQ * (2 * SEQ - 1)]  33.9 us
  transfers between devices with their start and end apart: 11, of which 10 were waited for; matrix products, arithmetic and copies ran while one was open for 14% of the time, Pallas kernels for 0%

commit v1 on v0

--- a/solution.py
+++ b/solution.py
@@ -4,6 +4,8 @@
 import jax.numpy as jnp
 import numpy as np
 from jax import lax
+from jax.experimental import pallas as pl
+from jax.experimental.pallas import tpu as pltpu
 from jax.sharding import PartitionSpec as P
 
 HEADS = 12
@@ -24,16 +26,108 @@
     return lax.ppermute(value, axis, [(source, source + steps) for source in range(first, last)])
 
 
-def offset_onehot(length, buckets):
+def bucket_starts(length, buckets):
     exact = buckets // 2
     distance = np.arange(length)
     far_bucket = exact + (
         np.log(np.maximum(distance, 1) / exact) / np.log(128.0 / exact) * (buckets - exact)
     ).astype(np.int64)
     near_table = np.where(distance < exact, distance, np.minimum(far_bucket, buckets - 1))
-    column = np.arange(2 * length)
-    column_bucket = near_table[np.maximum(length - 1 - column, 0)]
-    return (column_bucket[None, :] == np.arange(buckets)[:, None]).astype(np.float32)
+    return [int(np.argmax(near_table == bucket)) for bucket in range(buckets)]
+
+
+CHUNK = 64
+MESH = pl.DeviceIdType.MESH
+
+
+def line_sum_kernel(chunks, x_ref, out_ref, from_outer, from_inner, to_inner, send_sem, recv_sem):
+    stream, query, place = (lax.axis_index(name) for name in ("stream", "batch", "tensor"))
+    is_end = (place == 0) | (place == 3)
+    inner = (stream, query, jnp.where(place == 0, 1, jnp.where(place == 3, 2, 3 - place)))
+    outer = (stream, query, jnp.where(place == 1, 0, 3))
+    barrier = pltpu.get_barrier_semaphore()
+    pl.semaphore_signal(barrier, inc=1, device_id=inner, device_id_type=MESH)
+
+    @pl.when(is_end)
+    def _():
+        pl.semaphore_wait(barrier, 1)
+
+    @pl.when(jnp.logical_not(is_end))
+    def _():
+        pl.semaphore_signal(barrier, inc=1, device_id=outer, device_id_type=MESH)
+        pl.semaphore_wait(barrier, 2)
+
+    def rows(step):
+        return pl.ds(pl.multiple_of(step * CHUNK, CHUNK), CHUNK)
+
+    def to_middle(step):
+        return pltpu.make_async_remote_copy(
+            x_ref.at[rows(step)], from_outer.at[rows(step)], send_sem.at[0, step], recv_sem.at[0, step],
+            device_id=inner, device_id_type=MESH)
+
+    def across(step):
+        return pltpu.make_async_remote_copy(
+            to_inner.at[rows(step)], from_inner.at[rows(step)], send_sem.at[1, step], recv_sem.at[1, step],
+            device_id=inner, device_id_type=MESH)
+
+    def to_end(step):
+        return pltpu.make_async_remote_copy(
+            out_ref.at[rows(step)], out_ref.at[rows(step)], send_sem.at[2, step], recv_sem.at[2, step],
+            device_id=outer, device_id_type=MESH)
+
+    @pl.when(is_end)
+    def _():
+        @pl.loop(0, chunks)
+        def _(step):
+            to_middle(step).start()
+
+        @pl.loop(0, chunks)
+        def _(step):
+            to_middle(step).wait_send()
+            to_end(step).wait_recv()
+
+    @pl.when(jnp.logical_not(is_end))
+    def _():
+        def first(step):
+            to_middle(step).wait_recv()
+            to_inner[rows(step)] = (
+                from_outer[rows(step)].astype(jnp.float32) + x_ref[rows(step)].astype(jnp.float32)
+            ).astype(jnp.bfloat16)
+            across(step).start()
+
+        def second(step):
+            across(step).wait_recv()
+            out_ref[rows(step)] = (
+                from_inner[rows(step)].astype(jnp.float32) + to_inner[rows(step)].astype(jnp.float32)
+            ).astype(jnp.bfloat16)
+            to_end(step).start()
+
+        first(0)
+
+        @pl.loop(1, chunks)
+        def _(step):
+            first(step)
+            second(step - 1)
+
+        second(chunks - 1)
+
+        @pl.loop(0, chunks)
+        def _(step):
+            across(step).wait_send()
+            to_end(step).wait_send()
+
+
+def line_sum(value):
+    chunks = value.shape[0] // CHUNK
+    block = pltpu.VMEM(value.shape, jnp.bfloat16)
+    return pl.pallas_call(
+        partial(line_sum_kernel, chunks),
+        out_shape=jax.ShapeDtypeStruct(value.shape, jnp.bfloat16),
+        in_specs=[pl.BlockSpec(memory_space=pltpu.VMEM)],
+        out_specs=pl.BlockSpec(memory_space=pltpu.VMEM),
+        scratch_shapes=[block, block, block, pltpu.SemaphoreType.DMA((3, chunks)), pltpu.SemaphoreType.DMA((3, chunks))],
+        compiler_params=pltpu.CompilerParams(collective_id=0, has_side_effects=True, vmem_limit_bytes=32 * 2**20),
+    )(value.astype(jnp.bfloat16)).astype(jnp.float32)
 
 
 def layer_norm_forward(values, norm_gain, norm_shift):
@@ -185,18 +279,24 @@
     ).reshape(-1)
     packed_shift = jnp.where(is_first, packed_shift, 0.0)
     unit_shift = jnp.where(is_first, unit_bias, jnp.zeros_like(unit_bias))
-    onehot_cols = jnp.asarray(offset_onehot(SEQ, position_bias.shape[1]))
+    starts = bucket_starts(SEQ, position_bias.shape[1])
     position_f32 = position_bias.astype(jnp.float32)
+    apart = jnp.maximum(jnp.arange(SEQ)[:, None] - jnp.arange(SEQ)[None, :], 0)
 
     def lookup(table_values):
-        diagonal = jnp.dot(
-            table_values, onehot_cols, precision=HIGH, preferred_element_type=jnp.float32
-        )
-        repeated = jnp.tile(diagonal, (1, SEQ))
-        band = repeated[:, SEQ - 1 : SEQ - 1 + SEQ * (2 * SEQ - 1)].reshape(
-            table_values.shape[0], SEQ, 2 * SEQ - 1
-        )
-        return band[:, :, :SEQ]
+        band = jnp.broadcast_to(table_values[:, 0][:, None, None], (table_values.shape[0], SEQ, SEQ))
+        for bucket in range(1, len(starts)):
+            band = jnp.where(apart >= starts[bucket], table_values[:, bucket][:, None, None], band)
+        return band
+
+    def lookup_back(score_grads):
+        columns = []
+        for bucket in range(len(starts)):
+            inside = apart >= starts[bucket]
+            if bucket + 1 < len(starts):
+                inside = inside & (apart < starts[bucket + 1])
+            columns.append(jnp.sum(jnp.where(inside, score_grads, 0.0), axis=(1, 2)))
+        return jnp.stack(columns, axis=1)
 
     self_bias = jnp.where(is_first, 0.0, lookup(position_f32))
     enc_low = encodings.astype(jnp.bfloat16).reshape(total_rows, width)
@@ -218,10 +318,7 @@
     self_mixed, self_norm = lax.map(self_forward, (packed, passage_lengths, target_lengths))
     self_flat = self_mixed.reshape(total_rows, -1)
     attn_out = (
-        lax.psum(
-            jnp.dot(self_flat, proj_local, preferred_element_type=jnp.float32).astype(jnp.bfloat16),
-            "tensor",
-        ).astype(jnp.float32)
+        line_sum(jnp.dot(self_flat, proj_local, preferred_element_type=jnp.float32))
         + out_shift[0]
     )
     first_sum = source + attn_out
@@ -294,7 +391,7 @@
         cross_norm,
     ) = lax.cond(is_first, cross_skip, cross_run, middle)
     cross_total, mass_total = (
-        lax.psum(cross_part.astype(jnp.bfloat16), "tensor").astype(jnp.float32),
+        line_sum(cross_part),
         lax.psum(cross_mass.astype(jnp.bfloat16), "tensor").astype(jnp.float32),
     )
     second = middle + cross_total
@@ -304,10 +401,7 @@
         jnp.float32
     )
     act_low = jax.nn.gelu(pre_act, approximate=True).astype(jnp.bfloat16)
-    unit_out = lax.psum(
-        jnp.dot(act_low, down_local, preferred_element_type=jnp.float32).astype(jnp.bfloat16),
-        "tensor",
-    ).astype(jnp.float32)
+    unit_out = line_sum(jnp.dot(act_low, down_local, preferred_element_type=jnp.float32))
     unit_out = unit_out + out_shift[1]
     final_sum = second + unit_out
     final_norm, final_normed, final_root = layer_norm_forward(
@@ -345,10 +439,7 @@
     up_grad = jnp.dot(ffn_in.T, pre_grad, preferred_element_type=jnp.float32)
     down_grad = jnp.dot(act_low.T, unit_grad, preferred_element_type=jnp.float32)
     shift_grad = jnp.sum(pre_grad.astype(jnp.float32), axis=0)
-    ffn_in_grad = lax.psum(
-        jnp.dot(pre_grad, up_local.T, preferred_element_type=jnp.float32).astype(jnp.bfloat16),
-        "tensor",
-    ).astype(jnp.float32)
+    ffn_in_grad = line_sum(jnp.dot(pre_grad, up_local.T, preferred_element_type=jnp.float32))
     unit_pair = (up_grad, down_grad)
     ffn_back, rms_grad_three = rms_backward(second, ffn_root, gains[2], ffn_in_grad)
     second_grad = final_grad + jnp.where(is_first, ffn_in_grad, ffn_back)
@@ -398,7 +489,7 @@
     cross_in_part, cross_query_grad, cross_pair_grad, cross_proj_grad = lax.cond(
         is_first, cross_back_skip, cross_back_run, second_grad
     )
-    cross_in_grad = lax.psum(cross_in_part.astype(jnp.bfloat16), "tensor").astype(jnp.float32)
+    cross_in_grad = line_sum(cross_in_part)
     cross_back, rms_grad_two = rms_backward(middle, cross_root, gains[1], cross_in_grad)
     middle_grad = second_grad + jnp.where(is_first, 0.0, cross_back)
     first_back, gain_grad_one, shift_grad_one = layer_norm_backward(
@@ -413,7 +504,6 @@
         .astype(jnp.bfloat16)
         .reshape(query_count, SEQ, local_heads, HEAD_DIM)
     )
-    _, lookup_pull = jax.vjp(lookup, position_f32)
 
     def self_backward(query_items):
         packed_query, pass_lens, target_len, log_norm, grad_block = query_items
@@ -429,7 +519,7 @@
         )
         return (
             jnp.stack([grad_q, grad_k, grad_v], axis=2),
-            lookup_pull(grad_s.astype(jnp.float32))[0],
+            lookup_back(grad_s.astype(jnp.float32)),
         )
 
     packed_grad, table_grads = lax.map(
@@ -440,10 +530,7 @@
     qkv_weight_grad = jnp.dot(first_in.T, packed_grad, preferred_element_type=jnp.float32)
     shift_heads = jnp.sum(packed_grad.astype(jnp.float32), axis=0).reshape(local_heads, 3, HEAD_DIM)
     value_bias_grad = jnp.stack([shift_heads[:, 0], shift_heads[:, 2]], axis=1).reshape(-1)
-    first_in_grad = lax.psum(
-        jnp.dot(packed_grad, qkv_local.T, preferred_element_type=jnp.float32).astype(jnp.bfloat16),
-        "tensor",
-    ).astype(jnp.float32)
+    first_in_grad = line_sum(jnp.dot(packed_grad, qkv_local.T, preferred_element_type=jnp.float32))
     pre_back, rms_grad_one = rms_backward(source, pre_root, gains[0], first_in_grad)
     input_grad = first_grad + jnp.where(is_first, first_in_grad, pre_back)
     qkv_sum, proj_sum = sum_heads((qkv_weight_grad, proj_weight_grad))

time: 788 us -> 650 us (0.82)
  waiting for transfers between devices: 383 us -> 52.6 us
  Pallas kernels: 0 us -> 208 us
  local copies, waits for them, and re-layouts: 198 us -> 82.5 us
  other arithmetic: 102 us -> 152 us
  blocking collectives: 35.5 us -> 51.7 us
  matrix products: 36.4 us -> 51.8 us
  starting transfers between devices: 7.63 us -> 22.5 us
    psum x6 -> x0, waiting for transfers between devices: 300 us -> none  [the longest x1 73.7 us: local(): lax.psum(cross_part.astype(jnp.bfloat16), 'tensor').astype(jnp.float32)]
    pallas_call x0 -> x6, Pallas kernels: none -> 208 us  [line_sum(): pl.pallas_call(partial(line_sum_kernel, chunks), out_shape=jax.ShapeDtype...]
    unnamed x211 -> x403, local copies, waits for them, and re-layouts: 116 us -> 22.1 us
    another operation x12 -> x45, local copies, waits for them, and re-layouts: 8.59 us -> 45.3 us  [the longest x33 40 us: lookup_back(): return jnp.stack(columns, axis=1)]
    reshape x2 -> x0, local copies, waits for them, and re-layouts: 33.9 us -> none  [lookup(): repeated[:, SEQ - 1:SEQ - 1 + SEQ * (2 * SEQ - 1)]]
    ge x0 -> x31, other arithmetic: none -> 31.6 us  [lookup(): apart >= starts[bucket]]
    reduce_sum x1 -> x2, other arithmetic: 10.3 us -> 38.3 us  [lookup_back(): columns.append(jnp.sum(jnp.where(inside, score_grads, 0.0), axis=(1, 2)))]
    dot_general x1, matrix products: 1.93 us -> 26.5 us  [attend_scores(): jnp.einsum('ihd,jhd->hij', queries, key_heads, preferred_element_type=jnp...]
  transfers between devices with their start and end apart: 11 -> 5, of which waited for: 10 -> 2; matrix products, arithmetic and copies ran while one was open for 14% -> 15% of each run, Pallas kernels for 0% -> 0%
where the time goes in v1:
time: 650 us; the launch traced here: 641 us
  Pallas kernels  208 us (32%)
  other arithmetic  152 us (23%)
  local copies, waits for them, and re-layouts  82.5 us (13%)
  waiting for transfers between devices  52.6 us (8%)
  matrix products  51.8 us (8%)
  blocking collectives  51.7 us (8%)
  starting transfers between devices  22.5 us (3%)
  between operations  20.5 us (3%)
    pallas_call x6, Pallas kernels, line_sum(): pl.pallas_call(partial(line_sum_kernel, chunks), out_shape=jax.ShapeDtype...  208 us
    psum x1, waiting for transfers between devices, local(): lax.psum((side_terms[0], side_terms[1], side_terms[2], side_terms[3], sid...  48.5 us
    psum x1, blocking collectives, local(): lax.psum((side_terms[0], side_terms[1], side_terms[2], side_terms[3], sid...  40.7 us
    another operation x33, local copies, waits for them, and re-layouts, lookup_back(): return jnp.stack(columns, axis=1)  40 us
    reduce_sum x2, other arithmetic, lookup_back(): columns.append(jnp.sum(jnp.where(inside, score_grads, 0.0), axis=(1, 2)))  38.3 us
    ge x31, other arithmetic, lookup(): apart >= starts[bucket]  31.6 us
    dot_general x1, matrix products, attend_scores(): jnp.einsum('ihd,jhd->hij', queries, key_heads, preferred_element_type=jnp...  26.5 us
    ppermute x3, starting transfers between devices, from_behind(): lax.ppermute(value, axis, [(source, source + steps) for source in range(f...  22.4 us
  transfers between devices with their start and end apart: 5, of which 2 were waited for; matrix products, arithmetic and copies ran while one was open for 15% of the time, Pallas kernels for 0%

profile of v1, /device:TPU:0, one launch (start us, length us, event | category | flops | bytes accessed | tf_op | source)
XLA Modules:
  0.0 641.1 jit_solution(8785374539693453945)
XLA Ops:
  55.0 26.5 %fusion.260 = (f32[3,768]{1,0:T(4,128)S(1)}, f32[3,768,768]{1,2,0:T(8,128)S(1)}) fusion(f32[3]{0:T(128)S(1)} %copy-done.185, f32[3]{0:T(128)S(1)} %copy-done.186, pred[768,768]{0,1:T(8,128)(4,1)S(1)} %copy-done.70, f32[3]{0:T(128)S(1)} %copy-done.187, pred[768,768]{0,1:T(8,128)(4,1)S(1)} %copy-done.71, f32[3]{0:T(128)S(1)} %copy-done.188, ...), kind=kOutput, calls=%fused_computation.444 | convolution fusion | flops 290191104 | bytes 26567680 | tf_op jit(solution)/shard_map/while/body/eval_jaxpr/ihd,jhd->hij/dot_general | solution.py:186
  86.3 39.0 %shard_map.327 = bf16[768,768]{1,0:T(8,128)(2,1)S(1)} custom-call(bf16[768,768]{1,0:T(8,128)(2,1)S(1)} %convolution_convert_fusion.8.x_ref), custom_call_target="tpu_custom_call" | custom-call | tf_op jit(solution)/shard_map/pallas_call | solution.py:123
  130.3 5.0 conditional.2
  136.5 36.7 %shard_map.328 = bf16[768,768]{1,0:T(8,128)(2,1)S(1)} custom-call(bf16[768,768]{1,0:T(8,128)(2,1)} %get-tuple-element.188.x_ref), custom_call_target="tpu_custom_call" | custom-call | tf_op jit(solution)/shard_map/pallas_call | solution.py:123
  178.8 35.6 %shard_map.329 = bf16[768,768]{1,0:T(8,128)(2,1)S(1)} custom-call(bf16[768,768]{1,0:T(8,128)(2,1)S(1)} %convolution_convert_fusion.7.x_ref), custom_call_target="tpu_custom_call" | custom-call | tf_op jit(solution)/shard_map/pallas_call | solution.py:123
  217.9 3.2 convert_bitcast_fusion.1
  222.6 19.6 %collective-permute-start = (f32[1,2]{1,0:T(1,128)}, f32[1,2]{1,0:T(1,128)}, u32[]{:S(2)}, u32[]{:S(2)}) collective-permute-start(f32[1,2]{1,0:T(1,128)} %bitcast.50), channel_id=1, source_target_pairs={{0,16},{1,17},{2,18},{3,19},{4,20},{5,21},{6,22},{7,23},{8,24},{9,... | collective-permute-start | bytes 32 | tf_op jit(solution)/shard_map/ppermute | solution.py:26
  266.5 11.0 %psum.105 = bf16[1,2]{1,0:T(2,128)(2,1)} all-reduce(bf16[1,2]{1,0:T(2,128)(2,1)} %get-tuple-element.189), channel_id=1, replica_groups=mesh['stream'=2,'batch'=4,'tensor'=4] {'tensor'}, use_global_device_ids=true, to_apply=%region_19.20 | all-reduce | flops 2 | bytes 8 | tf_op jit(solution)/shard_map/psum | solution.py:395
  282.6 2.4 multiply_reduce_fusion.12
  289.7 4.0 collective-permute-done.2
  295.9 4.1 fusion.116
  301.8 3.0 convert_reduce_fusion.2
  306.9 32.8 %shard_map.330 = bf16[768,768]{1,0:T(8,128)(2,1)S(1)} custom-call(bf16[768,768]{1,0:T(8,128)(2,1)S(1)} %convolution_convert_fusion.6.x_ref), custom_call_target="tpu_custom_call" | custom-call | tf_op jit(solution)/shard_map/pallas_call | solution.py:123
  347.7 32.7 %shard_map.331 = bf16[768,768]{1,0:T(8,128)(2,1)S(1)} custom-call(bf16[768,768]{1,0:T(8,128)(2,1)} %copy-done.22), custom_call_target="tpu_custom_call" | custom-call | tf_op jit(solution)/shard_map/pallas_call | solution.py:123
  382.9 3.0 multiply_reduce_fusion.4
  393.8 20.9 %fusion.63 = (f32[3]{0:T(128)}, f32[3]{0:T(128)}, f32[3]{0:T(128)}, f32[3]{0:T(128)}, f32[3]{0:T(128)}, /*index=5*/f32[3]{0:T(128)}, f32[3]{0:T(128)}, f32[3]{0:...) fusion(pred[768,768]{0,1:T(8,128)(4,1)S(1)} %copy-done.37, ...), kind=kLoop, calls=%fused_computation.115 | loop fusion | flops 72548288 | bytes 28330200 | tf_op jit(solution)/shard_map/while/body/eval_jaxpr/reduce_sum | solution.py:298
  425.4 2.5 fusion.212
  427.9 30.8 %shard_map.332 = bf16[768,768]{1,0:T(8,128)(2,1)S(1)} custom-call(bf16[768,768]{1,0:T(8,128)(2,1)S(1)} %convolution_convert_fusion.5.x_ref), custom_call_target="tpu_custom_call" | custom-call | tf_op jit(solution)/shard_map/pallas_call | solution.py:123
  466.7 17.3 %fusion.62 = (f32[3]{0:T(128)}, f32[3]{0:T(128)}, f32[3]{0:T(128)}, f32[3]{0:T(128)}, f32[3]{0:T(128)}, /*index=5*/f32[3]{0:T(128)}, f32[3]{0:T(128)}, f32[3]{0:...) fusion(bf16[3,768,768]{1,2,0:T(8,128)(2,1)} %copy-done.7, ...), kind=kLoop, calls=%fused_computation.114 | loop fusion | flops 51314636 | bytes 11796648 | tf_op jit(solution)/shard_map/while/body/eval_jaxpr/reduce_sum | solution.py:298
  527.7 40.7 %all-reduce = (f32[384]{0:T(512)}, f32[768]{0:T(1024)}, f32[2,768]{1,0:T(2,128)}, f32[2,768]{1,0:T(2,128)}, f32[2,768]{1,0:T(2,128)}, /*index=5*/f32[3,768]{1,0:T(4,128)}, f32[3,32]{1,0:T(4,128)}) all-reduce(f32[384]{0:T(512)S(1)} %copy-done.166, ...), channel_id=1, replica_groups=mesh['stream'=2,'batch'=4,'tensor'=4] {'stream','batch'}, use_global_device_ids=true, to_apply=%region_37.38 | all-reduce | flops 8160 | bytes 65280 | tf_op jit(solution)/shard_map/psum | solution.py:568
  568.4 4.1 fusion.98
  572.5 2.6 broadcast_in_dim.807
  579.1 48.5 %all-reduce.6.cloned.1.call-done = (f32[768,192]{0,1:T(8,128)}, f32[768,384]{1,0:T(8,128)}, f32[192,768]{1,0:T(8,128)}) async-done(((f32[768,192]{0,1:T(8,128)}, f32[768,384]{1,0:T(8,128)}, f32[192,768]{1,0:T(8,128)}), (f32[768,192]{0,1:T(8,128)}, f32[768,384]{1,0:T(8,128)}, f32[192,768]{1,0:T(8,128)})) %all-reduce.6.cloned.1.call-update) | async-done | bytes 2359312 | tf_op jit(solution)/shard_map/psum | solution.py:568
  629.7 2.4 copy.287
  (606 shorter events, 197.3 us)
Async XLA Ops:
  7.2 170.0 %copy-start = (bf16[1,768,768]{2,1,0:T(8,128)(2,1)S(1)}, bf16[1,768,768]{2,1,0:T(8,128)(2,1)}, u32[]{:S(2)}) copy-start(bf16[1,768,768]{2,1,0:T(8,128)(2,1)} %param.29) | copy-start | bytes 3538948
  7.2 565.3 %all-reduce.8.cloned.1.call-start = ((), (), s32[]{:S(2)}) async-start(), calls=%async_computation.1 | async-start | bytes 7077888 | tf_op jit(solution)/shard_map/psum | solution.py:235
  42.8 85.3 %copy-start.83 = (f32[768]{0:T(1024)}, f32[768]{0:T(1024)S(1)}, u32[]{:S(2)}) copy-start(f32[768]{0:T(1024)S(1)} %get-tuple-element.376) | copy-start | bytes 9220
  54.7 27.9 %copy-start.68 = (bf16[768,576]{0,1:T(8,128)(2,1)}, bf16[768,576]{0,1:T(8,128)(2,1)S(1)}, u32[]{:S(2)}) copy-start(bf16[768,576]{0,1:T(8,128)(2,1)S(1)} %add_convert_fusion) | copy-start | bytes 2654212
  85.8 40.0 %copy-start.62 = (bf16[3,64,768]{2,1,0:T(8,128)(2,1)}, bf16[3,64,768]{2,1,0:T(8,128)(2,1)S(1)}, u32[]{:S(2)}) copy-start(bf16[3,64,768]{2,1,0:T(8,128)(2,1)S(1)} %fusion.219) | copy-start | bytes 884740
  136.5 36.7 %copy-start.3 = (f32[768,768]{1,0:T(8,128)S(1)}, f32[768,768]{1,0:T(8,128)}, u32[]{:S(2)}) copy-start(f32[768,768]{1,0:T(8,128)} %add_select_fusion.2) | copy-start | bytes 7077892
  173.7 40.7 %copy-start.10 = (f32[768,768]{1,0:T(8,128)}, f32[768,768]{1,0:T(8,128)S(1)}, u32[]{:S(2)}) copy-start(f32[768,768]{1,0:T(8,128)S(1)} %get-tuple-element.447) | copy-start | bytes 7077892
  178.8 35.6 %copy-start.122 = (f32[768]{0:T(1024)S(1)}, f32[768]{0:T(1024)}, u32[]{:S(2)}) copy-start(f32[768]{0:T(1024)} %get-tuple-element.379) | copy-start | bytes 9220
  222.6 56.2 %collective-permute-start = (f32[1,2]{1,0:T(1,128)}, f32[1,2]{1,0:T(1,128)}, u32[]{:S(2)}, u32[]{:S(2)}) collective-permute-start(f32[1,2]{1,0:T(1,128)} %bitcast.50), channel_id=1, source_target_pairs={{0,16},{1,17},{2,18},{3,19},{4,20},{5,21},{6,22},{7,23},{8,24},{9,... | collective-permute-start | bytes 32 | tf_op jit(solution)/shard_map/ppermute | solution.py:26
  286.9 8.2 %collective-permute-start.1 = (f32[1,2]{1,0:T(1,128)S(1)}, f32[1,2]{1,0:T(1,128)S(1)}, u32[]{:S(2)}, u32[]{:S(2)}) collective-permute-start(f32[1,2]{1,0:T(1,128)S(1)} %multiply_subtract_fusion), channel_id=1, source_target_pairs={{16,0},{17,1},{18,2},{19,3},{20,4},{21,5},{22,6},{23,7},{24,8},{25... | collective-permute-start | bytes 32 | tf_op jit(solution)/shard_map/ppermute | solution.py:26
  288.2 5.5 collective-permute-start.2
  301.8 39.5 %copy-start.18 = (f32[768,768]{1,0:T(8,128)}, f32[768,768]{1,0:T(8,128)S(1)}, u32[]{:S(2)}) copy-start(f32[768,768]{1,0:T(8,128)S(1)} %get-tuple-element.437) | copy-start | bytes 7077892
  305.8 34.0 %copy-start.101 = (f32[768]{0:T(1024)S(1)}, f32[768]{0:T(1024)}, u32[]{:S(2)}) copy-start(f32[768]{0:T(1024)} %copy-done.100) | copy-start | bytes 9220
  305.8 34.0 %copy-start.104 = (f32[768]{0:T(1024)S(1)}, f32[768]{0:T(1024)}, u32[]{:S(2)}) copy-start(f32[768]{0:T(1024)} %get-tuple-element.373) | copy-start | bytes 9220
  306.9 32.9 %copy-start.11 = (f32[768,768]{1,0:T(8,128)S(1)}, f32[768,768]{1,0:T(8,128)}, u32[]{:S(2)}) copy-start(f32[768,768]{1,0:T(8,128)} %copy-done.10) | copy-start | bytes 7077892
  347.7 32.8 %copy-start.4 = (f32[768,768]{1,0:T(8,128)S(1)}, f32[768,768]{1,0:T(8,128)}, u32[]{:S(2)}) copy-start(f32[768,768]{1,0:T(8,128)} %add_select_fusion.2) | copy-start | bytes 7077892
  347.7 32.8 %copy-start.106 = (f32[768]{0:T(1024)S(1)}, f32[768]{0:T(1024)}, u32[]{:S(2)}) copy-start(f32[768]{0:T(1024)} %get-tuple-element.372) | copy-start | bytes 9220
  387.8 33.3 %copy-start.13 = (f32[768,768]{1,0:T(8,128)}, f32[768,768]{1,0:T(8,128)S(1)}, u32[]{:S(2)}) copy-start(f32[768,768]{1,0:T(8,128)S(1)} %get-tuple-element.435) | copy-start | bytes 7077892
  466.6 161.1 %all-reduce.6.cloned.1.call-start = ((), (), s32[]{:S(2)}) async-start(), calls=%async_computation | async-start | bytes 4718592 | tf_op jit(solution)/shard_map/psum | solution.py:568
  466.6 39.2 %copy-start.179 = (f32[3]{0:T(128)S(1)}, f32[3]{0:T(128)}, u32[]{:S(2)}) copy-start(f32[3]{0:T(128)} %get-tuple-element.347) | copy-start | bytes 40
  466.6 56.6 %copy-start.178 = (f32[3]{0:T(128)S(1)}, f32[3]{0:T(128)}, u32[]{:S(2)}) copy-start(f32[3]{0:T(128)} %get-tuple-element.330) | copy-start | bytes 40
  466.7 57.3 %copy-start.24 = (f32[768,384]{0,1:T(8,128)S(1)}, f32[768,384]{0,1:T(8,128)}, u32[]{:S(2)}) copy-start(f32[768,384]{0,1:T(8,128)} %copy-done.23) | copy-start | bytes 3538948
  523.9 44.5 %copy-start.119 = (f32[768]{0:T(1024)S(1)}, f32[768]{0:T(1024)}, u32[]{:S(2)}) copy-start(f32[768]{0:T(1024)} %get-tuple-element.368) | copy-start | bytes 9220
  523.9 44.5 %copy-start.111 = (f32[768]{0:T(1024)S(1)}, f32[768]{0:T(1024)}, u32[]{:S(2)}) copy-start(f32[768]{0:T(1024)} %get-tuple-element.454) | copy-start | bytes 9220
  (181 other events, 672.9 us)
Sparse Core Ops, SparseCore 0:
  466.7 93.4 all-reduce.7
  564.2 63.3 all-reduce.5
